TPU v7x, 32 devices: a whole 2x2x4 slice. The times are simulated.
32 devices in a mesh: shot: 16 (over z, y, x), slab: 2 (over core).
Axes of the slice: x: 2, y: 2, z: 4, core: 2. Of those that a mesh axis runs over, the one named last changes fastest.
Arguments:
- velocity: float32 [16, 32, 32, 128], P('shot', None, 'slab'), may hold values from 0.15 to 0.45
- fwd_field: float32 [16, 64, 32, 256], P('shot', None, 'slab'), may hold values from -4 to 4
- adj_field: float32 [16, 64, 32, 256], P('shot', None, 'slab'), may hold values from -4 to 4
- aperture_anchor: int32 [16, 2], P('shot'), may hold values from 0 to 2, as said below
- source_cell: int32 [16, 16], P('shot'), may hold values from 0 to 524287
- wavelet: float32 [16, 2, 16], P('shot'), may hold values from -6 to 6
- shot_count: int32 [16], P('shot'), may hold values from 1 to 16
- receiver_cell: int32 [16, 1024], P('shot'), may hold values from 0 to 524287
- residual: float32 [16, 2, 1024], P('shot'), may hold values from -6 to 6
Outputs:
- gradient: float32 [16, 32, 32, 128], P('shot', None, 'slab')
Inputs may be any that keep to these rules, and one draw needn't show every extreme that they name: `aperture_anchor`: entry g, 0 is g // 4 or one less and entry g, 1 is g % 4 or one less, each clipped so that the 2 x 2 tiles of the aperture lie in the model.
All inputs are finite; a program needn't handle non-finite values.
Results may differ from a plain program's by a relative error of at most 0.0003.
Values sent between devices are 32-bit elements; how exact they have to be, the bound alone decides.
A program may use at most 64 MiB of HBM per device.

v0:
```python
import jax
import jax.numpy as jnp
from jax import lax
from jax.sharding import PartitionSpec as P

TILES_Y = 4


CENTRE = -205.0 / 72.0
STENCIL = (1.6, -0.2, 8.0 / 315.0, -1.0 / 560.0)
NEARBY = ((-1, -1), (-1, 0), (-1, 1), (0, -1), (0, 0), (0, 1), (1, -1), (1, 0), (1, 1))


def from_behind(value, axis, steps):
    count = lax.axis_size(axis)
    leading, last = (max(0, -steps), min(count, count - steps))
    return lax.ppermute(value, axis, [(source, source + steps) for source in range(leading, last)])


def padded_2(cells, sides, width):
    for axis, dim in sides:
        count = lax.axis_size(axis)
        ends = count - 1
        head = lax.slice_in_dim(cells, 0, width, axis=dim)
        tail = lax.slice_in_dim(cells, cells.shape[dim] - width, cells.shape[dim], axis=dim)
        cells = jnp.concatenate(
            [
                lax.ppermute(tail, axis, [(i, (i + 1) % count) for i in range(ends)]),
                cells,
                lax.ppermute(head, axis, [((i + 1) % count, i) for i in range(ends)]),
            ],
            axis=dim,
        )
    return cells


def laplace(padded_z):
    inner_depth = padded_z.shape[1] - 8
    padded = jnp.pad(padded_z, ((4, 4), (0, 0), (4, 4)))
    along_x = padded_z.shape[0]
    along_y = padded_z.shape[2]

    def window(shift_x, shift_z, shift_y):
        return padded[
            4 + shift_x : 4 + shift_x + along_x,
            4 + shift_z : 4 + shift_z + inner_depth,
            4 + shift_y : 4 + shift_y + along_y,
        ]

    summed = 3.0 * CENTRE * window(0, 0, 0)
    for distance in range(1, 5):
        paired = window(distance, 0, 0) + window(-distance, 0, 0)
        paired = paired + window(0, distance, 0) + window(0, -distance, 0)
        paired = paired + window(0, 0, distance) + window(0, 0, -distance)
        summed = summed + STENCIL[distance - 1] * paired
    return summed


def inject(field, positions, amounts, first_layer, total_depth):
    along_x = field.shape[0]
    depth = field.shape[1]
    plane_cells = field.shape[2]
    cell_x = positions // (total_depth * plane_cells)
    cell_z = positions // plane_cells % total_depth - first_layer
    cell_y = positions % plane_cells
    inside = (cell_z >= 0) & (cell_z < depth)
    row_index = cell_x * depth + cell_z
    row_ids = jnp.arange(along_x * depth, dtype=jnp.int32)
    rows_hot = ((row_ids[:, None] == row_index[None, :]) & inside[None, :]).astype(jnp.float32)
    col_ids = jnp.arange(plane_cells, dtype=jnp.int32)
    cols_hot = (cell_y[:, None] == col_ids[None, :]).astype(jnp.float32) * amounts[:, None]
    added = jnp.dot(
        rows_hot, cols_hot, precision=lax.Precision.HIGHEST, preferred_element_type=jnp.float32
    )
    return field + added.reshape(field.shape)


def fetch_tile(tile, step_row, step_col):
    return from_behind(tile, "shot", -(step_row * TILES_Y + step_col))


def return_tile(piece, step_row, step_col):
    return from_behind(piece, "shot", step_row * TILES_Y + step_col)


def body(
    velocity,
    fwd_field,
    adj_field,
    aperture_anchor,
    source_cell,
    wavelet,
    shot_count,
    receiver_cell,
    residual,
):
    own_tile = velocity[0]
    rows_x = own_tile.shape[0]
    depth_cells = own_tile.shape[1]
    cols_y = own_tile.shape[2]
    total_depth = depth_cells * lax.axis_size("slab")
    first_layer = lax.axis_index("slab") * depth_cells
    device = lax.axis_index("shot")
    home_row = device // TILES_Y
    home_col = device % TILES_Y
    anchor_row = aperture_anchor[0, 0]
    anchor_col = aperture_anchor[0, 1]
    gathered = []
    for step_row, step_col in NEARBY:
        if step_row == 0 and step_col == 0:
            gathered.append(own_tile)
        else:
            gathered.append(fetch_tile(own_tile, step_row, step_col))
    stacked = jnp.stack(gathered, 0)

    def place(part_row, part_col):
        return (anchor_row + part_row - home_row + 1) * 3 + (anchor_col + part_col - home_col + 1)

    halves = []
    for part_row in range(2):
        pair = [stacked[place(part_row, part_col)] for part_col in range(2)]
        halves.append(jnp.concatenate(pair, 2))
    speeds = jnp.concatenate(halves, 0)
    coefficient = speeds * speeds
    active = (jnp.arange(source_cell.shape[1], dtype=jnp.int32) < shot_count[0]).astype(jnp.float32)
    wide_coefficient = padded_2(coefficient, (("slab", 1),), 4)

    def advance(initial, positions, first_amounts, second_amounts):
        padded = padded_2(initial, (("slab", 1),), 8)
        first_wide = inject(
            wide_coefficient * laplace(padded),
            positions,
            first_amounts,
            first_layer - 4,
            total_depth,
        )
        middle = padded[:, 4:-4] + first_wide
        second_change = inject(
            coefficient * laplace(middle), positions, second_amounts, first_layer, total_depth
        )
        return (first_wide[:, 4:-4], second_change)

    first_change, second_change = advance(
        fwd_field[0], source_cell[0], wavelet[0, 0] * active, wavelet[0, 1] * active
    )
    start_adjoint = adj_field[0]
    back_first, back_second = advance(
        start_adjoint, receiver_cell[0], residual[0, 1], residual[0, 0]
    )
    later = start_adjoint + back_first
    earlier = 2.0 * later - start_adjoint + back_second
    imaged = earlier * first_change + later * second_change
    pieces = []
    for part_row in range(2):
        for part_col in range(2):
            block = imaged[
                part_row * rows_x : (part_row + 1) * rows_x,
                :,
                part_col * cols_y : (part_col + 1) * cols_y,
            ]
            pieces.append((part_row, part_col, block))
    nothing = jnp.zeros_like(own_tile)
    summed = nothing
    for step_row, step_col in NEARBY:
        outgoing = nothing
        for part_row, part_col, block in pieces:
            matches = (anchor_row + part_row - home_row == step_row) & (
                anchor_col + part_col - home_col == step_col
            )
            outgoing = outgoing + jnp.where(matches, block, 0.0)
        if step_row == 0 and step_col == 0:
            summed = summed + outgoing
        else:
            summed = summed + return_tile(outgoing, step_row, step_col)
    return (2.0 * own_tile * summed)[None]


def solution(mesh):
    placed = (
        P("shot", None, "slab", None),
        P("shot", None, "slab", None),
        P("shot", None, "slab", None),
        P("shot", None),
        P("shot", None),
        P("shot", None, None),
        P("shot"),
        P("shot", None),
        P("shot", None, None),
    )
    return jax.shard_map(
        body, mesh=mesh, in_specs=placed, out_specs=P("shot", None, "slab", None), check_vma=False
    )
```

profile of v0, /device:TPU:24, one launch (start us, length us, event | category | flops | bytes accessed | tf_op | source)
XLA Modules:
  0.0 138.1 jit_solution(17377976162697016013)
XLA Ops:
  0.0 1.4 %collective-permute-start = (f32[32,16,128]{2,1,0:T(8,128)}, f32[32,16,128]{2,1,0:T(8,128)}, u32[]{:S(2)}, u32[]{:S(2)}) collective-permute-start(f32[32,16,128]{2,1,0:T(8,128)} %bitcast.68), channel_id=1, source_target_pairs={{0,10},{2,12},{4,14},{6,16},{8,18},{10,20},{12,22},{14,24},{16,26}... | collective-permute-start | bytes 786440 | tf_op jit(solution)/shard_map/ppermute | solution.py:17
  1.4 1.3 collective-permute-start.1
  2.7 4.4 %collective-permute-start.2 = (f32[32,16,128]{2,1,0:T(8,128)}, f32[32,16,128]{2,1,0:T(8,128)}, u32[]{:S(2)}, u32[]{:S(2)}) collective-permute-start(f32[32,16,128]{2,1,0:T(8,128)} %bitcast.70), channel_id=1, source_target_pairs={{0,6},{2,8},{4,10},{6,12},{8,14},{10,16},{12,18},{14,20},{16,22},{... | collective-permute-start | bytes 786440 | tf_op jit(solution)/shard_map/ppermute | solution.py:17
  7.1 1.9 %collective-permute-start.3 = (f32[32,16,128]{2,1,0:T(8,128)}, f32[32,16,128]{2,1,0:T(8,128)S(1)}, u32[]{:S(2)}, u32[]{:S(2)}) collective-permute-start(f32[32,16,128]{2,1,0:T(8,128)} %bitcast.71), channel_id=1, source_target_pairs={{0,2},{2,4},{4,6},{6,8},{8,10},{10,12},{12,14},{14,16},{16,18},{18... | collective-permute-start | bytes 786440 | tf_op jit(solution)/shard_map/ppermute | solution.py:17
  9.0 5.7 %collective-permute-start.4 = (f32[32,16,128]{2,1,0:T(8,128)}, f32[32,16,128]{2,1,0:T(8,128)S(1)}, u32[]{:S(2)}, u32[]{:S(2)}) collective-permute-start(f32[32,16,128]{2,1,0:T(8,128)} %bitcast.72), channel_id=1, source_target_pairs={{2,0},{4,2},{6,4},{8,6},{10,8},{12,10},{14,12},{16,14},{18,16},{20... | collective-permute-start | bytes 786440 | tf_op jit(solution)/shard_map/ppermute | solution.py:17
  17.4 2.2 %fusion.170 = (f32[64,8,256]{2,1,0:T(8,128)}, f32[64,8,256]{2,1,0:T(8,128)}) fusion(f32[64,16,256]{2,1,0:T(8,128)} %bitcast.61), kind=kLoop, calls=%fused_computation.301 | loop fusion | bytes 2097152 | tf_op jit(solution)/shard_map/slice | solution.py:25
  21.0 4.6 %fusion.1 = f32[1536,256]{1,0:T(8,128)} fusion(s32[1024]{0:T(1024)S(1)} %bitcast.78, pred[1024]{0:T(1024)(128)(4,1)S(1)} %get-tuple-element.5, f32[1024]{0:T(1024)S(1)} %bitcast.80, s32[1024]{0:T(1024)S(1)} %add_select_fusion), kind=kOutput, calls=%fused_computation.66 | convolution fusion | flops 4835508224 | bytes 1586176 | tf_op jit(solution)/shard_map/dot_general | solution.py:72
  25.6 3.4 %fusion.4 = f32[1024,256]{1,0:T(8,128)} fusion(s32[1024]{0:T(1024)S(1)} %bitcast.77, pred[1024]{0:T(1024)(128)(4,1)S(1)} %get-tuple-element.6, f32[1024]{0:T(1024)S(1)} %bitcast.79, s32[1024]{0:T(1024)S(1)} %add_select_fusion), kind=kOutput, calls=%fused_computation.69 | convolution fusion | flops 3223846912 | bytes 1061888 | tf_op jit(solution)/shard_map/dot_general | solution.py:72
  29.8 1.6 %fusion.146 = f32[1024,256]{1,0:T(8,128)} fusion(s32[16]{0:T(128)S(1)} %add_bitcast_fusion, pred[16]{0:T(512)(128)(4,1)S(1)} %and_bitcast_fusion, f32[16]{0:T(128)S(1)} %get-tuple-element.39, s32[16]{0:T(128)S(1)} %and_select_fusion.3), kind=kOutput, calls=%fused_computation.221 | convolution fusion | flops 50372608 | bytes 1048784 | tf_op jit(solution)/shard_map/dot_general | solution.py:72
  34.6 2.9 %collective-permute-start.5 = (f32[32,16,128]{2,1,0:T(8,128)S(1)}, f32[32,16,128]{2,1,0:T(8,128)S(1)}, u32[]{:S(2)}, u32[]{:S(2)}) collective-permute-start(f32[32,16,128]{2,1,0:T(8,128)S(1)} %bitcast.73), channel_id=1, source_target_pairs={{6,0},{8,2},{10,4},{12,6},{14,8},{16,10},{18,12},{20,14},{22,16},{... | collective-permute-start | bytes 786440 | tf_op jit(solution)/shard_map/ppermute | solution.py:17
  38.6 4.4 %collective-permute-start.6 = (f32[32,16,128]{2,1,0:T(8,128)S(1)}, f32[32,16,128]{2,1,0:T(8,128)S(1)}, u32[]{:S(2)}, u32[]{:S(2)}) collective-permute-start(f32[32,16,128]{2,1,0:T(8,128)S(1)} %bitcast.74), channel_id=1, source_target_pairs={{8,0},{10,2},{12,4},{14,6},{16,8},{18,10},{20,12},{22,14},{24,16},... | collective-permute-start | bytes 786440 | tf_op jit(solution)/shard_map/ppermute | solution.py:17
  44.0 5.1 %collective-permute-start.7 = (f32[32,16,128]{2,1,0:T(8,128)S(1)}, f32[32,16,128]{2,1,0:T(8,128)S(1)}, u32[]{:S(2)}, u32[]{:S(2)}) collective-permute-start(f32[32,16,128]{2,1,0:T(8,128)S(1)} %bitcast.75), channel_id=1, source_target_pairs={{10,0},{12,2},{14,4},{16,6},{18,8},{20,10},{22,12},{24,14},{26,16}... | collective-permute-start | bytes 786440 | tf_op jit(solution)/shard_map/ppermute | solution.py:17
  50.1 1.3 collective-permute-start.12
  51.5 1.3 collective-permute-start.13
  52.8 3.1 %collective-permute-start.10 = (f32[64,8,256]{2,1,0:T(8,128)S(1)}, f32[64,8,256]{2,1,0:T(8,128)S(1)}, u32[]{:S(2)}, u32[]{:S(2)}) collective-permute-start(f32[64,8,256]{2,1,0:T(8,128)S(1)} %copy-done.11), channel_id=1, source_target_pairs={{0,1},{2,3},{4,5},{6,7},{8,9},{10,11},{12,13},{14,15},{16,17},{18,... | collective-permute-start | bytes 1572872 | tf_op jit(solution)/shard_map/ppermute | solution.py:28
  56.0 1.3 collective-permute-start.11
  58.3 3.1 %collective-permute-start.8 = (f32[64,4,256]{2,1,0:T(4,128)S(1)}, f32[64,4,256]{2,1,0:T(4,128)S(1)}, u32[]{:S(2)}, u32[]{:S(2)}) collective-permute-start(f32[64,4,256]{2,1,0:T(4,128)S(1)} %get-tuple-element.32), channel_id=1, source_target_pairs={{0,1},{2,3},{4,5},{6,7},{8,9},{10,11},{12,13},{14,15},{16,17},{18,... | collective-permute-start | bytes 786440 | tf_op jit(solution)/shard_map/ppermute | solution.py:28
  61.4 1.5 %collective-permute-start.9 = (f32[64,4,256]{2,1,0:T(4,128)S(1)}, f32[64,4,256]{2,1,0:T(4,128)S(1)}, u32[]{:S(2)}, u32[]{:S(2)}) collective-permute-start(f32[64,4,256]{2,1,0:T(4,128)S(1)} %get-tuple-element.33), channel_id=1, source_target_pairs={{1,0},{3,2},{5,4},{7,6},{9,8},{11,10},{13,12},{15,14},{17,16},{19,... | collective-permute-start | bytes 786440 | tf_op jit(solution)/shard_map/ppermute | solution.py:30
  63.3 1.5 %collective-permute-done.9 = f32[64,4,256]{2,1,0:T(4,128)S(1)} collective-permute-done((f32[64,4,256]{2,1,0:T(4,128)S(1)}, f32[64,4,256]{2,1,0:T(4,128)S(1)}, u32[]{:S(2)}, u32[]{:S(2)}) %collective-permute-start.9) | collective-permute-done | bytes 262176 | tf_op jit(solution)/shard_map/ppermute | solution.py:30
  64.8 6.3 %slice_add_fusion = (f32[64,24,256]{2,1,0:T(8,128)S(1)}, f32[64,24,256]{2,1,0:T(8,128)}) fusion(f32[64,32,256]{2,1,0:T(8,128)S(1)} %pad_maximum_fusion.1, f32[64,24,256]{2,1,0:T(8,128)S(1)} %bitcast.64, f32[64,16,256]{2,1,0:T(8,128)S(1)} %bitcast.63, f32[64,8,256]{2,1,0:T(8,128)S(1)} %collective-permute-done.12, ...), kind=kLoop, calls=%fused_computation.137 | loop fusion | flops 14155776 | bytes 21495808 | tf_op jit(solution)/shard_map/add | solution.py:137
  71.1 6.3 %slice_add_fusion.1 = (f32[64,24,256]{2,1,0:T(8,128)S(1)}, f32[64,24,256]{2,1,0:T(8,128)}) fusion(f32[64,32,256]{2,1,0:T(8,128)S(1)} %pad_maximum_fusion, f32[64,24,256]{2,1,0:T(8,128)S(1)} %bitcast.66, f32[64,16,256]{2,1,0:T(8,128)S(1)} %bitcast.60, f32[64,8,256]{2,1,0:T(8,128)S(1)} %collective-permute-done.10, ...), kind=kLoop, calls=%fused_computation.138 | loop fusion | flops 14155776 | bytes 21495808 | tf_op jit(solution)/shard_map/add | solution.py:137
  77.4 10.7 %fusion.84 = f32[64,16,256]{2,1,0:T(8,128)} fusion(f32[64,16,256]{2,1,0:T(8,128)} %bitcast.67, f32[64,24,256]{2,1,0:T(8,128)S(1)} %get-tuple-element.13, f32[64,16,256]{2,1,0:T(8,128)} %bitcast.65, f32[64,24,256]{2,1,0:T(8,128)S(1)} %get-tuple-element.7, f32[64,24,256]{2,1,0:T(8,128)} %get-tuple-element.8, f32[64,24,256]{2,1,0:T(8,128)} %get-tuple-element.14, ...), kind=kLoop, calls=%fused_computation.153 | loop fusion | flops 19136512 | bytes 29360128 | tf_op jit(solution)/shard_map/add | solution.py:152
  88.1 2.1 %select_add_fusion.7 = (f32[32,16,128]{2,1,0:T(8,128)S(1)}, f32[32,16,128]{2,1,0:T(8,128)}) fusion(f32[64,16,256]{2,1,0:T(8,128)} %fusion.84, pred[]{:T(512)S(6)} %and.295, pred[]{:T(512)S(6)} %and.294, pred[]{:T(512)S(6)} %and.293, pred[]{:T(512)S(6)} %and.268, pred[]{:T(512)S(6)} %and.319, pred[]{:T(512)S(6)} %and.318, pred[]{:T(512)S(6)} %and.317, ...), kind=kLoop, calls=%fused_computation.240 | loop fusion | flops 917504 | bytes 1572872 | tf_op jit(solution)/shard_map/add | solution.py:170
  90.2 2.0 %collective-permute-start.14 = (f32[32,16,128]{2,1,0:T(8,128)S(1)}, f32[32,16,128]{2,1,0:T(8,128)S(1)}, u32[]{:S(2)}, u32[]{:S(2)}) collective-permute-start(f32[32,16,128]{2,1,0:T(8,128)S(1)} %get-tuple-element.24), channel_id=1, source_target_pairs={{10,0},{12,2},{14,4},{16,6},{18,8},{20,10},{22,12},{24,14},{26,16}... | collective-permute-start | bytes 786440 | tf_op jit(solution)/shard_map/ppermute | solution.py:17
  92.3 9.4 %collective-permute-start.15 = (f32[32,16,128]{2,1,0:T(8,128)S(1)}, f32[32,16,128]{2,1,0:T(8,128)S(1)}, u32[]{:S(2)}, u32[]{:S(2)}) collective-permute-start(f32[32,16,128]{2,1,0:T(8,128)S(1)} %get-tuple-element.22), channel_id=1, source_target_pairs={{8,0},{10,2},{12,4},{14,6},{16,8},{18,10},{20,12},{22,14},{24,16},... | collective-permute-start | bytes 786440 | tf_op jit(solution)/shard_map/ppermute | solution.py:17
  101.8 1.9 %collective-permute-start.18 = (f32[32,16,128]{2,1,0:T(8,128)S(1)}, f32[32,16,128]{2,1,0:T(8,128)S(1)}, u32[]{:S(2)}, u32[]{:S(2)}) collective-permute-start(f32[32,16,128]{2,1,0:T(8,128)S(1)} %get-tuple-element.23), channel_id=1, source_target_pairs={{0,2},{2,4},{4,6},{6,8},{8,10},{10,12},{12,14},{14,16},{16,18},{18... | collective-permute-start | bytes 786440 | tf_op jit(solution)/shard_map/ppermute | solution.py:17
  103.7 2.1 %collective-permute-start.19 = (f32[32,16,128]{2,1,0:T(8,128)}, f32[32,16,128]{2,1,0:T(8,128)S(1)}, u32[]{:S(2)}, u32[]{:S(2)}) collective-permute-start(f32[32,16,128]{2,1,0:T(8,128)} %get-tuple-element.25), channel_id=1, source_target_pairs={{0,6},{2,8},{4,10},{6,12},{8,14},{10,16},{12,18},{14,20},{16,22},{... | collective-permute-start | bytes 786440 | tf_op jit(solution)/shard_map/ppermute | solution.py:17
  106.7 4.8 %collective-permute-start.16 = (f32[32,16,128]{2,1,0:T(8,128)}, f32[32,16,128]{2,1,0:T(8,128)S(1)}, u32[]{:S(2)}, u32[]{:S(2)}) collective-permute-start(f32[32,16,128]{2,1,0:T(8,128)} %get-tuple-element.26), channel_id=1, source_target_pairs={{6,0},{8,2},{10,4},{12,6},{14,8},{16,10},{18,12},{20,14},{22,16},{... | collective-permute-start | bytes 786440 | tf_op jit(solution)/shard_map/ppermute | solution.py:17
  113.8 6.3 %collective-permute-start.17 = (f32[32,16,128]{2,1,0:T(8,128)}, f32[32,16,128]{2,1,0:T(8,128)S(1)}, u32[]{:S(2)}, u32[]{:S(2)}) collective-permute-start(f32[32,16,128]{2,1,0:T(8,128)} %get-tuple-element.28), channel_id=1, source_target_pairs={{2,0},{4,2},{6,4},{8,6},{10,8},{12,10},{14,12},{16,14},{18,16},{20... | collective-permute-start | bytes 786440 | tf_op jit(solution)/shard_map/ppermute | solution.py:17
  121.5 3.1 %collective-permute-done.16 = f32[32,16,128]{2,1,0:T(8,128)S(1)} collective-permute-done((f32[32,16,128]{2,1,0:T(8,128)}, f32[32,16,128]{2,1,0:T(8,128)S(1)}, u32[]{:S(2)}, u32[]{:S(2)}) %collective-permute-start.16) | collective-permute-done | bytes 262176 | tf_op jit(solution)/shard_map/ppermute | solution.py:17
  124.6 4.1 %collective-permute-done.17 = f32[32,16,128]{2,1,0:T(8,128)S(1)} collective-permute-done((f32[32,16,128]{2,1,0:T(8,128)}, f32[32,16,128]{2,1,0:T(8,128)S(1)}, u32[]{:S(2)}, u32[]{:S(2)}) %collective-permute-start.17) | collective-permute-done | bytes 262176 | tf_op jit(solution)/shard_map/ppermute | solution.py:17
  128.7 8.5 %collective-permute-done.21 = f32[32,16,128]{2,1,0:T(8,128)S(1)} collective-permute-done((f32[32,16,128]{2,1,0:T(8,128)}, f32[32,16,128]{2,1,0:T(8,128)S(1)}, u32[]{:S(2)}, u32[]{:S(2)}) %collective-permute-start.21) | collective-permute-done | bytes 262176 | tf_op jit(solution)/shard_map/ppermute | solution.py:17
  (84 shorter events, 14.6 us)
Async XLA Ops:
  0.0 19.7 %copy-start.12 = (s32[1,1024]{1,0:T(1,128)S(1)}, s32[1,1024]{1,0:T(1,128)}, u32[]{:S(2)}) copy-start(s32[1,1024]{1,0:T(1,128)} %param.16) | copy-start | bytes 12292
  0.0 19.8 %copy-start.13 = (f32[1,2,1024]{2,1,0:T(2,128)S(1)}, f32[1,2,1024]{2,1,0:T(2,128)}, u32[]{:S(2)}) copy-start(f32[1,2,1024]{2,1,0:T(2,128)} %param.17) | copy-start | bytes 24580
  0.0 19.8 %copy-start.1 = (f32[1,64,16,256]{3,2,1,0:T(8,128)S(1)}, f32[1,64,16,256]{3,2,1,0:T(8,128)}, u32[]{:S(2)}) copy-start(f32[1,64,16,256]{3,2,1,0:T(8,128)} %param.11) | copy-start | bytes 3145732
  0.0 34.6 %collective-permute-start = (f32[32,16,128]{2,1,0:T(8,128)}, f32[32,16,128]{2,1,0:T(8,128)}, u32[]{:S(2)}, u32[]{:S(2)}) collective-permute-start(f32[32,16,128]{2,1,0:T(8,128)} %bitcast.68), channel_id=1, source_target_pairs={{0,10},{2,12},{4,14},{6,16},{8,18},{10,20},{12,22},{14,24},{16,26}... | collective-permute-start | bytes 786440 | tf_op jit(solution)/shard_map/ppermute | solution.py:17
  1.4 37.1 %collective-permute-start.1 = (f32[32,16,128]{2,1,0:T(8,128)}, f32[32,16,128]{2,1,0:T(8,128)}, u32[]{:S(2)}, u32[]{:S(2)}) collective-permute-start(f32[32,16,128]{2,1,0:T(8,128)} %bitcast.69), channel_id=1, source_target_pairs={{0,8},{2,10},{4,12},{6,14},{8,16},{10,18},{12,20},{14,22},{16,24},... | collective-permute-start | bytes 786440 | tf_op jit(solution)/shard_map/ppermute | solution.py:17
  2.7 41.2 %collective-permute-start.2 = (f32[32,16,128]{2,1,0:T(8,128)}, f32[32,16,128]{2,1,0:T(8,128)}, u32[]{:S(2)}, u32[]{:S(2)}) collective-permute-start(f32[32,16,128]{2,1,0:T(8,128)} %bitcast.70), channel_id=1, source_target_pairs={{0,6},{2,8},{4,10},{6,12},{8,14},{10,16},{12,18},{14,20},{16,22},{... | collective-permute-start | bytes 786440 | tf_op jit(solution)/shard_map/ppermute | solution.py:17
  7.1 42.9 %collective-permute-start.3 = (f32[32,16,128]{2,1,0:T(8,128)}, f32[32,16,128]{2,1,0:T(8,128)S(1)}, u32[]{:S(2)}, u32[]{:S(2)}) collective-permute-start(f32[32,16,128]{2,1,0:T(8,128)} %bitcast.71), channel_id=1, source_target_pairs={{0,2},{2,4},{4,6},{6,8},{8,10},{10,12},{12,14},{14,16},{16,18},{18... | collective-permute-start | bytes 786440 | tf_op jit(solution)/shard_map/ppermute | solution.py:17
  9.0 42.4 %collective-permute-start.4 = (f32[32,16,128]{2,1,0:T(8,128)}, f32[32,16,128]{2,1,0:T(8,128)S(1)}, u32[]{:S(2)}, u32[]{:S(2)}) collective-permute-start(f32[32,16,128]{2,1,0:T(8,128)} %bitcast.72), channel_id=1, source_target_pairs={{2,0},{4,2},{6,4},{8,6},{10,8},{12,10},{14,12},{16,14},{18,16},{20... | collective-permute-start | bytes 786440 | tf_op jit(solution)/shard_map/ppermute | solution.py:17
  28.9 5.7 %copy-start.8 = (f32[1,32,16,128]{3,2,1,0:T(8,128)S(1)}, f32[1,32,16,128]{3,2,1,0:T(8,128)}, u32[]{:S(2)}) copy-start(f32[1,32,16,128]{3,2,1,0:T(8,128)} %param.9) | copy-start | bytes 786436
  34.6 18.2 %copy-start.11 = (f32[64,8,256]{2,1,0:T(8,128)S(1)}, f32[64,8,256]{2,1,0:T(8,128)}, u32[]{:S(2)}) copy-start(f32[64,8,256]{2,1,0:T(8,128)} %get-tuple-element.34) | copy-start | bytes 1572868
  34.6 18.2 %collective-permute-start.5 = (f32[32,16,128]{2,1,0:T(8,128)S(1)}, f32[32,16,128]{2,1,0:T(8,128)S(1)}, u32[]{:S(2)}, u32[]{:S(2)}) collective-permute-start(f32[32,16,128]{2,1,0:T(8,128)S(1)} %bitcast.73), channel_id=1, source_target_pairs={{6,0},{8,2},{10,4},{12,6},{14,8},{16,10},{18,12},{20,14},{22,16},{... | collective-permute-start | bytes 786440 | tf_op jit(solution)/shard_map/ppermute | solution.py:17
  38.5 17.4 %copy-start.10 = (f32[64,8,256]{2,1,0:T(8,128)S(1)}, f32[64,8,256]{2,1,0:T(8,128)}, u32[]{:S(2)}) copy-start(f32[64,8,256]{2,1,0:T(8,128)} %get-tuple-element.35) | copy-start | bytes 1572868
  38.6 17.4 %collective-permute-start.6 = (f32[32,16,128]{2,1,0:T(8,128)S(1)}, f32[32,16,128]{2,1,0:T(8,128)S(1)}, u32[]{:S(2)}, u32[]{:S(2)}) collective-permute-start(f32[32,16,128]{2,1,0:T(8,128)S(1)} %bitcast.74), channel_id=1, source_target_pairs={{8,0},{10,2},{12,4},{14,6},{16,8},{18,10},{20,12},{22,14},{24,16},... | collective-permute-start | bytes 786440 | tf_op jit(solution)/shard_map/ppermute | solution.py:17
  44.0 13.3 %collective-permute-start.7 = (f32[32,16,128]{2,1,0:T(8,128)S(1)}, f32[32,16,128]{2,1,0:T(8,128)S(1)}, u32[]{:S(2)}, u32[]{:S(2)}) collective-permute-start(f32[32,16,128]{2,1,0:T(8,128)S(1)} %bitcast.75), channel_id=1, source_target_pairs={{10,0},{12,2},{14,4},{16,6},{18,8},{20,10},{22,12},{24,14},{26,16}... | collective-permute-start | bytes 786440 | tf_op jit(solution)/shard_map/ppermute | solution.py:17
  50.1 11.3 %collective-permute-start.12 = (f32[64,8,256]{2,1,0:T(8,128)}, f32[64,8,256]{2,1,0:T(8,128)S(1)}, u32[]{:S(2)}, u32[]{:S(2)}) collective-permute-start(f32[64,8,256]{2,1,0:T(8,128)} %get-tuple-element.30), channel_id=1, source_target_pairs={{0,1},{2,3},{4,5},{6,7},{8,9},{10,11},{12,13},{14,15},{16,17},{18,... | collective-permute-start | bytes 1572872 | tf_op jit(solution)/shard_map/ppermute | solution.py:28
  51.5 11.4 %collective-permute-start.13 = (f32[64,8,256]{2,1,0:T(8,128)}, f32[64,8,256]{2,1,0:T(8,128)S(1)}, u32[]{:S(2)}, u32[]{:S(2)}) collective-permute-start(f32[64,8,256]{2,1,0:T(8,128)} %get-tuple-element.31), channel_id=1, source_target_pairs={{1,0},{3,2},{5,4},{7,6},{9,8},{11,10},{13,12},{15,14},{17,16},{19,... | collective-permute-start | bytes 1572872 | tf_op jit(solution)/shard_map/ppermute | solution.py:30
  52.8 10.3 %collective-permute-start.10 = (f32[64,8,256]{2,1,0:T(8,128)S(1)}, f32[64,8,256]{2,1,0:T(8,128)S(1)}, u32[]{:S(2)}, u32[]{:S(2)}) collective-permute-start(f32[64,8,256]{2,1,0:T(8,128)S(1)} %copy-done.11), channel_id=1, source_target_pairs={{0,1},{2,3},{4,5},{6,7},{8,9},{10,11},{12,13},{14,15},{16,17},{18,... | collective-permute-start | bytes 1572872 | tf_op jit(solution)/shard_map/ppermute | solution.py:28
  56.0 7.1 %collective-permute-start.11 = (f32[64,8,256]{2,1,0:T(8,128)S(1)}, f32[64,8,256]{2,1,0:T(8,128)S(1)}, u32[]{:S(2)}, u32[]{:S(2)}) collective-permute-start(f32[64,8,256]{2,1,0:T(8,128)S(1)} %copy-done.10), channel_id=1, source_target_pairs={{1,0},{3,2},{5,4},{7,6},{9,8},{11,10},{13,12},{15,14},{17,16},{19,... | collective-permute-start | bytes 1572872 | tf_op jit(solution)/shard_map/ppermute | solution.py:30
  57.4 5.4 %copy-start.3 = (f32[1,64,16,256]{3,2,1,0:T(8,128)S(1)}, f32[1,64,16,256]{3,2,1,0:T(8,128)}, u32[]{:S(2)}) copy-start(f32[1,64,16,256]{3,2,1,0:T(8,128)} %param.10) | copy-start | bytes 3145732
  58.3 5.0 %collective-permute-start.8 = (f32[64,4,256]{2,1,0:T(4,128)S(1)}, f32[64,4,256]{2,1,0:T(4,128)S(1)}, u32[]{:S(2)}, u32[]{:S(2)}) collective-permute-start(f32[64,4,256]{2,1,0:T(4,128)S(1)} %get-tuple-element.32), channel_id=1, source_target_pairs={{0,1},{2,3},{4,5},{6,7},{8,9},{10,11},{12,13},{14,15},{16,17},{18,... | collective-permute-start | bytes 786440 | tf_op jit(solution)/shard_map/ppermute | solution.py:28
  61.4 3.4 %collective-permute-start.9 = (f32[64,4,256]{2,1,0:T(4,128)S(1)}, f32[64,4,256]{2,1,0:T(4,128)S(1)}, u32[]{:S(2)}, u32[]{:S(2)}) collective-permute-start(f32[64,4,256]{2,1,0:T(4,128)S(1)} %get-tuple-element.33), channel_id=1, source_target_pairs={{1,0},{3,2},{5,4},{7,6},{9,8},{11,10},{13,12},{15,14},{17,16},{19,... | collective-permute-start | bytes 786440 | tf_op jit(solution)/shard_map/ppermute | solution.py:30
  64.8 6.3 %copy-start.2 = (f32[1,64,16,256]{3,2,1,0:T(8,128)S(1)}, f32[1,64,16,256]{3,2,1,0:T(8,128)}, u32[]{:S(2)}) copy-start(f32[1,64,16,256]{3,2,1,0:T(8,128)} %param.11) | copy-start | bytes 3145732
  64.8 6.3 %copy-start.7 = (f32[1536,256]{1,0:T(8,128)S(1)}, f32[1536,256]{1,0:T(8,128)}, u32[]{:S(2)}) copy-start(f32[1536,256]{1,0:T(8,128)} %fusion.1) | copy-start | bytes 4718596
  90.2 22.3 %collective-permute-start.14 = (f32[32,16,128]{2,1,0:T(8,128)S(1)}, f32[32,16,128]{2,1,0:T(8,128)S(1)}, u32[]{:S(2)}, u32[]{:S(2)}) collective-permute-start(f32[32,16,128]{2,1,0:T(8,128)S(1)} %get-tuple-element.24), channel_id=1, source_target_pairs={{10,0},{12,2},{14,4},{16,6},{18,8},{20,10},{22,12},{24,14},{26,16}... | collective-permute-start | bytes 786440 | tf_op jit(solution)/shard_map/ppermute | solution.py:17
  92.3 21.4 %collective-permute-start.15 = (f32[32,16,128]{2,1,0:T(8,128)S(1)}, f32[32,16,128]{2,1,0:T(8,128)S(1)}, u32[]{:S(2)}, u32[]{:S(2)}) collective-permute-start(f32[32,16,128]{2,1,0:T(8,128)S(1)} %get-tuple-element.22), channel_id=1, source_target_pairs={{8,0},{10,2},{12,4},{14,6},{16,8},{18,10},{20,12},{22,14},{24,16},... | collective-permute-start | bytes 786440 | tf_op jit(solution)/shard_map/ppermute | solution.py:17
  101.8 18.4 %collective-permute-start.18 = (f32[32,16,128]{2,1,0:T(8,128)S(1)}, f32[32,16,128]{2,1,0:T(8,128)S(1)}, u32[]{:S(2)}, u32[]{:S(2)}) collective-permute-start(f32[32,16,128]{2,1,0:T(8,128)S(1)} %get-tuple-element.23), channel_id=1, source_target_pairs={{0,2},{2,4},{4,6},{6,8},{8,10},{10,12},{12,14},{14,16},{16,18},{18... | collective-permute-start | bytes 786440 | tf_op jit(solution)/shard_map/ppermute | solution.py:17
  103.7 33.5 %copy-start.9 = (f32[1,32,16,128]{3,2,1,0:T(8,128)S(1)}, f32[1,32,16,128]{3,2,1,0:T(8,128)}, u32[]{:S(2)}) copy-start(f32[1,32,16,128]{3,2,1,0:T(8,128)} %param.9) | copy-start | bytes 786436
  103.7 17.7 %collective-permute-start.19 = (f32[32,16,128]{2,1,0:T(8,128)}, f32[32,16,128]{2,1,0:T(8,128)S(1)}, u32[]{:S(2)}, u32[]{:S(2)}) collective-permute-start(f32[32,16,128]{2,1,0:T(8,128)} %get-tuple-element.25), channel_id=1, source_target_pairs={{0,6},{2,8},{4,10},{6,12},{8,14},{10,16},{12,18},{14,20},{16,22},{... | collective-permute-start | bytes 786440 | tf_op jit(solution)/shard_map/ppermute | solution.py:17
  106.7 17.9 %collective-permute-start.16 = (f32[32,16,128]{2,1,0:T(8,128)}, f32[32,16,128]{2,1,0:T(8,128)S(1)}, u32[]{:S(2)}, u32[]{:S(2)}) collective-permute-start(f32[32,16,128]{2,1,0:T(8,128)} %get-tuple-element.26), channel_id=1, source_target_pairs={{6,0},{8,2},{10,4},{12,6},{14,8},{16,10},{18,12},{20,14},{22,16},{... | collective-permute-start | bytes 786440 | tf_op jit(solution)/shard_map/ppermute | solution.py:17
  112.5 12.1 %collective-permute-start.20 = (f32[32,16,128]{2,1,0:T(8,128)}, f32[32,16,128]{2,1,0:T(8,128)S(1)}, u32[]{:S(2)}, u32[]{:S(2)}) collective-permute-start(f32[32,16,128]{2,1,0:T(8,128)} %get-tuple-element.27), channel_id=1, source_target_pairs={{0,8},{2,10},{4,12},{6,14},{8,16},{10,18},{12,20},{14,22},{16,24},... | collective-permute-start | bytes 786440 | tf_op jit(solution)/shard_map/ppermute | solution.py:17
  113.8 14.9 %collective-permute-start.17 = (f32[32,16,128]{2,1,0:T(8,128)}, f32[32,16,128]{2,1,0:T(8,128)S(1)}, u32[]{:S(2)}, u32[]{:S(2)}) collective-permute-start(f32[32,16,128]{2,1,0:T(8,128)} %get-tuple-element.28), channel_id=1, source_target_pairs={{2,0},{4,2},{6,4},{8,6},{10,8},{12,10},{14,12},{16,14},{18,16},{20... | collective-permute-start | bytes 786440 | tf_op jit(solution)/shard_map/ppermute | solution.py:17
  120.1 17.1 %collective-permute-start.21 = (f32[32,16,128]{2,1,0:T(8,128)}, f32[32,16,128]{2,1,0:T(8,128)S(1)}, u32[]{:S(2)}, u32[]{:S(2)}) collective-permute-start(f32[32,16,128]{2,1,0:T(8,128)} %get-tuple-element.29), channel_id=1, source_target_pairs={{0,10},{2,12},{4,14},{6,16},{8,18},{10,20},{12,22},{14,24},{16,26}... | collective-permute-start | bytes 786440 | tf_op jit(solution)/shard_map/ppermute | solution.py:17
  (6 other events, 10.2 us)
where the time goes:
time: 139 us; the launch traced here: 138 us
  starting transfers between devices  67.8 us (49%)
  other arithmetic  30.9 us (22%)
  waiting for transfers between devices  17.3 us (12%)
  matrix products  10.4 us (7%)
  local copies, waits for them, and re-layouts  7.82 us (6%)
  between operations  3.88 us (3%)
    ppermute x16, starting transfers between devices, from_behind(): lax.ppermute(value, axis, [(source, source + steps) for source in range(l...  56.3 us
    ppermute x16, waiting for transfers between devices, from_behind(): lax.ppermute(value, axis, [(source, source + steps) for source in range(l...  15.8 us
    add x2, other arithmetic, advance(): middle = padded[:, 4:-4] + first_wide  12.6 us
    add x1, other arithmetic, body(): imaged = earlier * first_change + later * second_change  10.7 us
    dot_general x4, matrix products, inject(): jnp.dot(rows_hot, cols_hot, precision=lax.Precision.HIGHEST, preferred_el...  10.4 us
    ppermute x3, starting transfers between devices, padded_2(): lax.ppermute(tail, axis, [(i, (i + 1) % count) for i in range(ends)])  7.48 us
    add x4, other arithmetic, body(): outgoing = outgoing + jnp.where(matches, block, 0.0)  4.12 us
    ppermute x3, starting transfers between devices, padded_2(): lax.ppermute(head, axis, [((i + 1) % count, i) for i in range(ends)])  4.06 us
  transfers between devices with their start and end apart: 22, of which 4 were waited for; matrix products, arithmetic and copies ran while one was open for 16% of the time, Pallas kernels for 0%

commit v1 on v0

v1 whole, which is shorter than its diff:
```python
import functools

import jax
import jax.numpy as jnp
import ml_dtypes
import numpy as np
from jax import lax
from jax.experimental import pallas as pl
from jax.experimental.pallas import tpu as pltpu
from jax.sharding import PartitionSpec as P

TILES_Y = 4
CENTRE = -205.0 / 72.0
STENCIL = (1.6, -0.2, 8.0 / 315.0, -1.0 / 560.0)
XB = 8
HALO = 8
MESH = pl.DeviceIdType.MESH
F32 = jnp.float32
BF16 = jnp.bfloat16


def split_matrix(values):
    high = values.astype(np.float32).astype(ml_dtypes.bfloat16)
    low = (values - high.astype(np.float64)).astype(np.float32).astype(ml_dtypes.bfloat16)
    return np.stack([high, low])


def stencil_matrices(depth, plane):
    weight = {0: 0.0}
    for distance in range(1, 5):
        weight[distance] = weight[-distance] = STENCIL[distance - 1]
    left = np.zeros((XB, depth, XB + 8, depth))
    beside = np.zeros((XB, depth, XB, depth))
    for x in range(XB):
        for z in range(depth):
            left[x, z, x + 4, z] += 3.0 * CENTRE
            for step in range(-4, 5):
                if step == 0:
                    continue
                left[x, z, x + 4 + step, z] += weight[step]
                if 0 <= z + step < depth:
                    left[x, z, x + 4, z + step] += weight[step]
                elif z + step < 0:
                    beside[x, z, x, z + step + depth] += weight[step]
                else:
                    beside[x, z, x, z + step - depth] += weight[step]
    right = np.zeros((plane, plane))
    for step in range(-4, 5):
        if step:
            right += weight[step] * np.eye(plane, k=step)
    rows = XB * depth
    return (
        split_matrix(left.reshape(rows, (XB + 8) * depth)),
        split_matrix(beside.reshape(rows, rows)),
        split_matrix(right),
    )


def dot(a, b):
    return jnp.dot(a, b, preferred_element_type=F32)


def dot3(a, b):
    return dot(a[0], b[0]) + dot(a[1], b[0]) + dot(a[0], b[1])


def kernel(
    shots,
    slabs,
    vel,
    fwd,
    adj,
    anchor,
    source,
    wavelet,
    count,
    receiver,
    residual,
    left_m,
    beside_m,
    right_m,
    out,
    field_h,
    field_l,
    halo,
    halo_h,
    halo_l,
    lap,
    inj,
    hot,
    flag_own,
    flag_up,
    flag_down,
    side,
    straight,
    picked,
    forward,
    moved,
    send_row,
    got_row,
    send_col,
    got_col,
    own_sum,
    slab_send,
    slab_recv,
    flag_send,
    flag_recv,
    side_send,
    side_recv,
    straight_send,
    straight_recv,
    picked_send,
    picked_recv,
    row_send,
    row_recv,
    col_send,
    col_recv,
):
    tile_x, depth, tile_y = vel.shape[1:]
    along_x, plane = fwd.shape[1], fwd.shape[3]
    blocks = along_x // XB
    chunks = tile_x // XB
    rows = XB * depth
    me = lax.axis_index("shot")
    layer = lax.axis_index("slab")
    home_row = me // TILES_Y
    home_col = me % TILES_Y
    has = {
        "left": home_col > 0,
        "right": home_col < TILES_Y - 1,
        "up": home_row > 0,
        "down": home_row < shots // TILES_Y - 1,
        "above": layer > 0,
        "below": layer < slabs - 1,
    }
    where = {
        "left": {"shot": me - 1},
        "right": {"shot": me + 1},
        "up": {"shot": me - TILES_Y},
        "down": {"shot": me + TILES_Y},
        "above": {"slab": layer - 1},
        "below": {"slab": layer + 1},
    }
    opposite = {
        "left": "right",
        "right": "left",
        "up": "down",
        "down": "up",
        "above": "below",
        "below": "above",
    }

    def copy_to(side_name, src, dst, send_sem, recv_sem):
        return pltpu.make_async_remote_copy(
            src_ref=src,
            dst_ref=dst,
            send_sem=send_sem,
            recv_sem=recv_sem,
            device_id=where[side_name],
            device_id_type=MESH,
        )

    def start(side_name, *parts):
        @pl.when(has[side_name])
        def _():
            copy_to(side_name, *parts).start()

    def arrived(side_name, *parts):
        source_side = opposite[side_name]

        @pl.when(has[source_side])
        def _():
            copy_to(source_side, *parts).wait_recv()

    def sent(side_name, *parts):
        @pl.when(has[side_name])
        def _():
            copy_to(side_name, *parts).wait_send()

    row_up = (home_row - anchor[0, 0]).astype(F32)
    col_left = (home_col - anchor[0, 1]).astype(F32)
    flag_own[...] = jnp.full(flag_own.shape, col_left, F32)

    for name in has:

        @pl.when(has[name])
        def _(name=name):
            pl.semaphore_signal(
                pltpu.get_barrier_semaphore(), inc=1, device_id=where[name], device_id_type=MESH
            )

    @pl.when(jnp.logical_not(has["above"]))
    def _():
        halo[:, :, HALO:, :] = jnp.zeros((4, along_x, HALO, plane), F32)

    @pl.when(jnp.logical_not(has["below"]))
    def _():
        halo[:, :, :HALO, :] = jnp.zeros((4, along_x, HALO, plane), F32)

    for index, name in enumerate(("up", "down")):

        @pl.when(jnp.logical_not(has[name]))
        def _(index=index):
            got_row[index] = jnp.zeros(got_row.shape[1:], F32)

    for index, name in enumerate(("left", "right")):

        @pl.when(jnp.logical_not(has[name]))
        def _(index=index):
            got_col[index] = jnp.zeros(got_col.shape[1:], F32)

    edge = jnp.zeros((2, 4, depth, plane), BF16)
    field_h[:, :4] = edge
    field_l[:, :4] = edge
    field_h[:, along_x + 4 :] = edge
    field_l[:, along_x + 4 :] = edge

    total = sum(has[name].astype(jnp.int32) for name in has)
    pl.semaphore_wait(pltpu.get_barrier_semaphore(), total)

    def slab_copy(name, index, src):
        layers = slice(0, HALO) if name == "above" else slice(depth - HALO, depth)
        way = 0 if name == "above" else 1
        return (
            name,
            src.at[:, layers, :],
            halo.at[index, :, layers, :],
            slab_send.at[index, way],
            slab_recv.at[index, way],
        )

    def flag_copy(name):
        dst = flag_down if name == "up" else flag_up
        way = 0 if name == "up" else 1
        return (name, flag_own, dst, flag_send.at[way], flag_recv.at[way])

    def chunk_of(k):
        return pl.ds(k * XB, XB)

    def side_copy(name, k):
        way = 0 if name == "right" else 1
        return (
            name,
            vel.at[0, chunk_of(k)],
            side.at[way, chunk_of(k)],
            side_send.at[way, k],
            side_recv.at[way, k],
        )

    def straight_copy(name):
        way = 0 if name == "down" else 1
        return (name, vel.at[0], straight.at[way], straight_send.at[way], straight_recv.at[way])

    def picked_copy(name, k):
        way = 0 if name == "down" else 1
        return (
            name,
            forward.at[way, chunk_of(k)],
            picked.at[way, chunk_of(k)],
            picked_send.at[way, k],
            picked_recv.at[way, k],
        )

    def row_copy(name, part, k):
        way = 0 if name == "down" else 1
        return (
            name,
            send_row.at[way, part, chunk_of(k)],
            got_row.at[way, part, chunk_of(k)],
            row_send.at[way, part, k],
            row_recv.at[way, part, k],
        )

    def col_copy(name, k):
        way = 0 if name == "right" else 1
        return (
            name,
            send_col.at[way, chunk_of(k)],
            got_col.at[way, chunk_of(k)],
            col_send.at[way, k],
            col_recv.at[way, k],
        )

    for name in ("up", "down"):
        start(*flag_copy(name))
    for k in range(chunks):
        for name in ("left", "right"):
            start(*side_copy(name, k))
        if k == 0:
            for index, src in enumerate((fwd.at[0], adj.at[0])):
                for name in ("above", "below"):
                    start(*slab_copy(name, index, src))
            for name in ("up", "down"):
                start(*straight_copy(name))

    def mask_of(flag_value, shape):
        return jnp.broadcast_to(flag_value, shape) > 0.5

    def split_to(high_ref, low_ref, index, at, value):
        high = value.astype(BF16)
        high_ref[index, at] = high
        low_ref[index, at] = (value - high.astype(F32)).astype(BF16)

    def split_field(index, src):
        @pl.loop(0, blocks)
        def _(b):
            split_to(field_h, field_l, index, pl.ds(b * XB + 4, XB), src[0, pl.ds(b * XB, XB)])

    def split_halo(index):
        @pl.loop(0, blocks)
        def _(b):
            at = pl.ds(b * XB, XB)
            split_to(halo_h, halo_l, index % 2, at, halo[index, at])

    def laplace(index, b):
        wide = pl.ds(b * XB, XB + 8)
        shape = ((XB + 8) * depth, plane)
        block = (field_h[index, wide].reshape(shape), field_l[index, wide].reshape(shape))
        at = pl.ds(b * XB, XB)
        near = (halo_h[index, at].reshape(rows, plane), halo_l[index, at].reshape(rows, plane))
        inner = tuple(part[4 * depth : 4 * depth + rows] for part in block)
        summed = dot3((left_m[0], left_m[1]), block)
        summed = summed + dot3((beside_m[0], beside_m[1]), near)
        summed = summed + dot3(inner, (right_m[0], right_m[1]))
        return summed.reshape(XB, depth, plane)

    def first_laplace(index):
        @pl.loop(0, blocks)
        def _(b):
            lap[index, pl.ds(b * XB, XB)] = laplace(index, b)

    first_layer = layer * depth
    total_depth = depth * slabs

    def whole_part(value, divisor):
        return ((value.astype(F32) + 0.5) * (1.0 / divisor)).astype(jnp.int32)

    def injections(index, positions, amounts):
        lanes = positions.shape[1]
        line = whole_part(positions, plane)
        cell_y = positions - line * plane
        cell_x = whole_part(line, total_depth)
        cell_z = line - cell_x * total_depth - first_layer
        inside = (cell_z >= 0) & (cell_z < depth)
        row_index = jnp.where(inside, cell_x * depth + cell_z, -1)
        col_hot = lax.broadcasted_iota(jnp.int32, (plane, lanes), 0) == cell_y
        for step in range(2):
            amount = amounts[step]
            high = amount.astype(BF16).astype(F32)
            for part, value in enumerate((high, amount - high)):
                at = (2 * step + part) * plane
                hot[at : at + plane, :lanes] = jnp.where(col_hot, value, 0.0).astype(BF16)
        tall = 2 * rows

        @pl.loop(0, along_x * depth // tall)
        def _(b):
            ids = lax.broadcasted_iota(jnp.int32, (tall, lanes), 0) + b * tall
            rows_hot = jnp.where(ids == row_index, 1.0, 0.0).astype(BF16)
            for step in range(2):
                cols = hot[2 * step * plane : 2 * (step + 1) * plane, :lanes]
                both = lax.dot_general(
                    rows_hot, cols, (((1,), (1,)), ((), ())), preferred_element_type=F32
                )
                added = both[:, :plane] + both[:, plane:]
                inj[2 * index + step, pl.ds(b * 2 * XB, 2 * XB)] = added.reshape(
                    2 * XB, depth, plane
                )

    def pass_on(k):
        for name in ("left", "right"):
            arrived(*side_copy(name, k))
        if k == 0:
            for name in ("up", "down"):
                arrived(*flag_copy(name))
        for way, flag in ((1, flag_up), (0, flag_down)):
            picks = mask_of(flag[...][None], (XB, depth, tile_y))
            forward[way, chunk_of(k)] = jnp.where(picks, side[0, chunk_of(k)], side[1, chunk_of(k)])
        for name in ("up", "down"):
            start(*picked_copy(name, k))

    split_field(0, fwd)
    split_field(1, adj)
    lane = lax.broadcasted_iota(jnp.int32, source.shape, 1)
    active = jnp.where(lane < count[0], 1.0, 0.0)
    injections(0, source[...], (wavelet[0, 0:1] * active, wavelet[0, 1:2] * active))
    pass_on(0)
    for index in range(2):
        for name in ("above", "below"):
            arrived(*slab_copy(name, index, (fwd, adj)[index].at[0]))
        split_halo(index)
    first_laplace(0)
    pass_on(1)
    injections(1, receiver[...], (residual[0, 1:2], residual[0, 0:1]))
    pass_on(2)
    first_laplace(1)
    pass_on(3)
    for k in range(4, chunks):
        pass_on(k)
    for name in ("up", "down"):
        arrived(*straight_copy(name))
        for k in range(chunks):
            arrived(*picked_copy(name, k))

    shape = (XB, depth, tile_y)
    is_left = mask_of(jnp.full(shape, col_left, F32), shape)
    is_up = mask_of(jnp.full(shape, row_up, F32), shape)

    def coefficient(part_row, k):
        at = chunk_of(k)
        own_same, own_other = vel[0, at], jnp.where(is_left, side[0, at], side[1, at])
        same, other = straight[part_row, at], picked[part_row, at]
        own_here = is_up if part_row == 1 else jnp.logical_not(is_up)
        same = jnp.where(own_here, own_same, same)
        other = jnp.where(own_here, own_other, other)
        speeds = jnp.concatenate(
            [jnp.where(is_left, other, same), jnp.where(is_left, same, other)], axis=2
        )
        return speeds * speeds

    for part_row in range(2):

        @pl.loop(0, chunks)
        def _(k):
            squares = coefficient(part_row, k)
            x = part_row * tile_x + k * XB
            at = pl.ds(x, XB)
            for index, src in enumerate((fwd, adj)):
                change = squares * lap[index, at] + inj[2 * index, at]
                lap[index, at] = change
                later = src[0, at] + change
                moved[index, at] = later
                split_to(field_h, field_l, index, pl.ds(x + 4, XB), later)

    for index in range(2):
        for name in ("above", "below"):
            start(*slab_copy(name, 2 + index, moved.at[index]))
    for index in range(2):
        for name in ("above", "below"):
            arrived(*slab_copy(name, 2 + index, moved.at[index]))
        split_halo(2 + index)

    def image(part_row, k):
        squares = coefficient(part_row, k)
        x = part_row * tile_x + k * XB
        b = part_row * chunks + k
        at = pl.ds(x, XB)
        second = squares * laplace(0, b) + inj[1, at]
        back = squares * laplace(1, b) + inj[3, at]
        later = moved[1, at]
        earlier = 2.0 * later - adj[0, at] + back
        whole = earlier * lap[0, at] + later * second
        low, high = whole[:, :, :tile_y], whole[:, :, tile_y:]
        return jnp.where(is_left, high, low), jnp.where(is_left, low, high)

    for k in range(chunks):
        at = chunk_of(k)
        first_same, first_other = image(0, k)
        last_same, last_other = image(1, k)
        send_row[1, 0, at] = jnp.where(is_up, first_other, 0.0)
        send_row[0, 0, at] = jnp.where(is_up, 0.0, last_other)
        send_row[1, 1, at] = jnp.where(is_up, first_same, 0.0)
        send_row[0, 1, at] = jnp.where(is_up, 0.0, last_same)
        for part in range(2):
            for name in ("up", "down"):
                start(*row_copy(name, part, k))
        own_sum[at] = jnp.where(is_up, last_same, first_same)
        own_other = jnp.where(is_up, last_other, first_other)
        send_col[1, at] = jnp.where(is_left, own_other, 0.0)
        send_col[0, at] = jnp.where(is_left, 0.0, own_other)

    for k in range(chunks):
        at = chunk_of(k)
        for name in ("up", "down"):
            arrived(*row_copy(name, 0, k))
        for way, flag in ((0, flag_up), (1, flag_down)):
            picks = mask_of(flag[...][None], shape)
            piece = got_row[way, 0, at]
            send_col[1, at] = send_col[1, at] + jnp.where(picks, piece, 0.0)
            send_col[0, at] = send_col[0, at] + jnp.where(picks, 0.0, piece)
        for name in ("left", "right"):
            start(*col_copy(name, k))
    for k in range(chunks):
        at = chunk_of(k)
        for name in ("up", "down"):
            arrived(*row_copy(name, 1, k))
        for name in ("left", "right"):
            arrived(*col_copy(name, k))
        summed = own_sum[at] + got_row[0, 1, at] + got_row[1, 1, at]
        out[0, at] = 2.0 * vel[0, at] * (summed + got_col[0, at] + got_col[1, at])

    for name in ("up", "down"):
        sent(*flag_copy(name))
        sent(*straight_copy(name))
        for k in range(chunks):
            sent(*picked_copy(name, k))
            for part in range(2):
                sent(*row_copy(name, part, k))
    for name in ("left", "right"):
        for k in range(chunks):
            sent(*side_copy(name, k))
            sent(*col_copy(name, k))
    for index in range(2):
        for name in ("above", "below"):
            sent(*slab_copy(name, index, (fwd, adj)[index].at[0]))
            sent(*slab_copy(name, 2 + index, moved.at[index]))


def body(shots, slabs, velocity, fwd_field, adj_field, anchor, source, wavelet, count, receiver, residual):
    tile_x, depth, tile_y = velocity.shape[1:]
    along_x, plane = fwd_field.shape[1], fwd_field.shape[3]
    chunks = tile_x // XB
    left_m, beside_m, right_m = (jnp.asarray(m) for m in stencil_matrices(depth, plane))
    vmem = pl.BlockSpec(memory_space=pltpu.VMEM)
    smem = pl.BlockSpec(memory_space=pltpu.SMEM)
    aperture = (along_x, depth, plane)
    tile = (tile_x, depth, tile_y)
    dma = pltpu.SemaphoreType.DMA
    lanes = receiver.shape[1]
    return pl.pallas_call(
        functools.partial(kernel, shots, slabs),
        out_shape=jax.ShapeDtypeStruct(velocity.shape, F32),
        in_specs=[vmem, vmem, vmem, smem, vmem, vmem, smem, vmem, vmem, vmem, vmem, vmem],
        out_specs=vmem,
        scratch_shapes=[
            pltpu.VMEM((2, along_x + 8, depth, plane), BF16),
            pltpu.VMEM((2, along_x + 8, depth, plane), BF16),
            pltpu.VMEM((4,) + aperture, F32),
            pltpu.VMEM((2,) + aperture, BF16),
            pltpu.VMEM((2,) + aperture, BF16),
            pltpu.VMEM((2,) + aperture, F32),
            pltpu.VMEM((4,) + aperture, F32),
            pltpu.VMEM((4 * plane, lanes), BF16),
            pltpu.VMEM((depth, tile_y), F32),
            pltpu.VMEM((depth, tile_y), F32),
            pltpu.VMEM((depth, tile_y), F32),
            pltpu.VMEM((2,) + tile, F32),
            pltpu.VMEM((2,) + tile, F32),
            pltpu.VMEM((2,) + tile, F32),
            pltpu.VMEM((2,) + tile, F32),
            pltpu.VMEM((2,) + aperture, F32),
            pltpu.VMEM((2, 2) + tile, F32),
            pltpu.VMEM((2, 2) + tile, F32),
            pltpu.VMEM((2,) + tile, F32),
            pltpu.VMEM((2,) + tile, F32),
            pltpu.VMEM(tile, F32),
            dma((4, 2)),
            dma((4, 2)),
            dma((2,)),
            dma((2,)),
            dma((2, chunks)),
            dma((2, chunks)),
            dma((2,)),
            dma((2,)),
            dma((2, chunks)),
            dma((2, chunks)),
            dma((2, 2, chunks)),
            dma((2, 2, chunks)),
            dma((2, chunks)),
            dma((2, chunks)),
        ],
        compiler_params=pltpu.CompilerParams(
            collective_id=0, has_side_effects=True, vmem_limit_bytes=48 * 1024 * 1024
        ),
    )(
        velocity, fwd_field, adj_field, anchor, source, wavelet, count, receiver, residual,
        left_m, beside_m, right_m,
    )


def solution(mesh):
    placed = (
        P("shot", None, "slab", None),
        P("shot", None, "slab", None),
        P("shot", None, "slab", None),
        P("shot", None),
        P("shot", None),
        P("shot", None, None),
        P("shot"),
        P("shot", None),
        P("shot", None, None),
    )
    return jax.shard_map(
        functools.partial(body, mesh.shape["shot"], mesh.shape["slab"]),
        mesh=mesh,
        in_specs=placed,
        out_specs=P("shot", None, "slab", None),
        check_vma=False,
    )
```

time: 139 us -> 51.1 us (0.37)
  the two profiles are of different devices: /device:TPU:24 before, /device:TPU:3 now
where the time goes in v1:
time: 51.1 us; the launch traced here: 50.7 us
  Pallas kernels  41.2 us (81%)
  local copies, waits for them, and re-layouts  8.83 us (17%)
  between operations  0.72 us (1%)
    pallas_call x1, Pallas kernels, body(): pl.pallas_call(functools.partial(kernel, shots, slabs), out_shape=jax.Sha...  41.2 us
    unnamed x23, local copies, waits for them, and re-layouts  8.83 us

profile of v1, /device:TPU:3, one launch (start us, length us, event | category | flops | bytes accessed | tf_op | source)
XLA Modules:
  0.0 50.7 jit_solution(18031821804574267455)
XLA Ops:
  0.0 0.0 copy-start.8
  0.0 0.0 copy-start.9
  0.7 0.0 copy-done.8
  0.7 0.0 copy-done.9
  0.7 0.0 copy-start
  0.7 1.2 %copy-done = f32[1,64,16,256]{3,2,1,0:T(8,128)S(1)} copy-done((f32[1,64,16,256]{3,2,1,0:T(8,128)S(1)}, f32[1,64,16,256]{3,2,1,0:T(8,128)}, u32[]{:S(2)}) %copy-start) | copy-done | bytes 1048600
  1.9 0.0 copy-start.1
  1.9 1.2 %copy-done.1 = f32[1,64,16,256]{3,2,1,0:T(8,128)S(1)} copy-done((f32[1,64,16,256]{3,2,1,0:T(8,128)S(1)}, f32[1,64,16,256]{3,2,1,0:T(8,128)}, u32[]{:S(2)}) %copy-start.1) | copy-done | bytes 1048600
  3.2 0.0 copy-start.2
  3.2 0.9 %copy-done.2 = f32[1,32,16,128]{3,2,1,0:T(8,128)S(1)} copy-done((f32[1,32,16,128]{3,2,1,0:T(8,128)S(1)}, f32[1,32,16,128]{3,2,1,0:T(8,128)}, u32[]{:S(2)}) %copy-start.2) | copy-done | bytes 262168
  4.1 0.0 copy-start.3
  4.1 0.9 %copy-done.3 = bf16[2,256,256]{2,1,0:T(8,128)(2,1)S(1)} copy-done((bf16[2,256,256]{2,1,0:T(8,128)(2,1)S(1)}, bf16[2,256,256]{2,1,0:T(8,128)(2,1)}, u32[]{:S(2)}) %copy-start.3) | copy-done | bytes 262168
  5.1 0.0 copy-start.4
  5.1 0.9 %copy-done.4 = bf16[2,128,256]{2,1,0:T(8,128)(2,1)S(1)} copy-done((bf16[2,128,256]{2,1,0:T(8,128)(2,1)S(1)}, bf16[2,128,256]{2,1,0:T(8,128)(2,1)}, u32[]{:S(2)}) %copy-start.4) | copy-done | bytes 131096
  6.0 0.0 copy-start.5
  6.0 0.8 %copy-done.5 = bf16[2,128,128]{2,1,0:T(8,128)(2,1)S(1)} copy-done((bf16[2,128,128]{2,1,0:T(8,128)(2,1)S(1)}, bf16[2,128,128]{2,1,0:T(8,128)(2,1)}, u32[]{:S(2)}) %copy-start.5) | copy-done | bytes 65560
  6.8 0.0 copy-start.6
  6.8 0.7 %copy-done.6 = f32[1,2,1024]{2,1,0:T(2,128)S(1)} copy-done((f32[1,2,1024]{2,1,0:T(2,128)S(1)}, f32[1,2,1024]{2,1,0:T(2,128)}, u32[]{:S(2)}) %copy-start.6) | copy-done | bytes 8216
  7.5 0.0 copy-start.7
  7.5 0.7 %copy-done.7 = s32[1,1024]{1,0:T(1,128)S(1)} copy-done((s32[1,1024]{1,0:T(1,128)S(1)}, s32[1,1024]{1,0:T(1,128)}, u32[]{:S(2)}) %copy-start.7) | copy-done | bytes 4120
  8.2 0.0 copy-start.10
  8.2 0.7 %copy-done.10 = s32[1,16]{1,0:T(1,128)S(1)} copy-done((s32[1,16]{1,0:T(1,128)S(1)}, s32[1,16]{1,0:T(1,128)}, u32[]{:S(2)}) %copy-start.10) | copy-done | bytes 88
  8.8 41.2 %shard_map.118 = f32[1,32,16,128]{3,2,1,0:T(8,128)S(1)} custom-call(f32[1,32,16,128]{3,2,1,0:T(8,128)S(1)} %copy-done.2, f32[1,64,16,256]{3,2,1,0:T(8,128)S(1)} %copy-done, f32[1,64,16,256]{3,2,1,0:T(8,128)S(1)} %copy-done.1, s32[1,2]{1,0:T(1,128)S(1)} %copy-done.9, s32[1,16]{1,0:T(1,128)S(1)} %copy-done.10, f32[1,2,16]{2,1,0:T(2,128)S(1)} %copy-done.8, ...), custom_call_target="tpu_custom_call" | custom-call | tf_op jit(solution)/shard_map/pallas_call | solution.py:519
  50.0 0.7 %copy.15 = f32[1,32,16,128]{3,2,1,0:T(8,128)} copy(f32[1,32,16,128]{3,2,1,0:T(8,128)S(1)} %shard_map.118) | data formatting | bytes 524288
Async XLA Ops:
  0.0 0.7 %copy-start.8 = (f32[1,2,16]{2,1,0:T(2,128)S(1)}, f32[1,2,16]{2,1,0:T(2,128)}, u32[]{:S(2)}) copy-start(f32[1,2,16]{2,1,0:T(2,128)} %wavelet.1) | copy-start | bytes 388
  0.0 0.7 %copy-start.9 = (s32[1,2]{1,0:T(1,128)S(1)}, s32[1,2]{1,0:T(1,128)}, u32[]{:S(2)}) copy-start(s32[1,2]{1,0:T(1,128)} %anchor.1) | copy-start | bytes 28
  0.7 1.2 %copy-start = (f32[1,64,16,256]{3,2,1,0:T(8,128)S(1)}, f32[1,64,16,256]{3,2,1,0:T(8,128)}, u32[]{:S(2)}) copy-start(f32[1,64,16,256]{3,2,1,0:T(8,128)} %fwd.1) | copy-start | bytes 3145732
  1.9 1.2 %copy-start.1 = (f32[1,64,16,256]{3,2,1,0:T(8,128)S(1)}, f32[1,64,16,256]{3,2,1,0:T(8,128)}, u32[]{:S(2)}) copy-start(f32[1,64,16,256]{3,2,1,0:T(8,128)} %adj.1) | copy-start | bytes 3145732
  3.2 0.9 %copy-start.2 = (f32[1,32,16,128]{3,2,1,0:T(8,128)S(1)}, f32[1,32,16,128]{3,2,1,0:T(8,128)}, u32[]{:S(2)}) copy-start(f32[1,32,16,128]{3,2,1,0:T(8,128)} %vel.1) | copy-start | bytes 786436
  4.1 0.9 %copy-start.3 = (bf16[2,256,256]{2,1,0:T(8,128)(2,1)S(1)}, bf16[2,256,256]{2,1,0:T(8,128)(2,1)}, u32[]{:S(2)}) copy-start(bf16[2,256,256]{2,1,0:T(8,128)(2,1)} %constant.8.clone.right_m) | copy-start | bytes 786436
  5.1 0.9 %copy-start.4 = (bf16[2,128,256]{2,1,0:T(8,128)(2,1)S(1)}, bf16[2,128,256]{2,1,0:T(8,128)(2,1)}, u32[]{:S(2)}) copy-start(bf16[2,128,256]{2,1,0:T(8,128)(2,1)} %constant.6.clone.left_m) | copy-start | bytes 393220
  6.0 0.8 %copy-start.5 = (bf16[2,128,128]{2,1,0:T(8,128)(2,1)S(1)}, bf16[2,128,128]{2,1,0:T(8,128)(2,1)}, u32[]{:S(2)}) copy-start(bf16[2,128,128]{2,1,0:T(8,128)(2,1)} %constant.7.clone.beside_m) | copy-start | bytes 196612
  6.8 0.7 %copy-start.6 = (f32[1,2,1024]{2,1,0:T(2,128)S(1)}, f32[1,2,1024]{2,1,0:T(2,128)}, u32[]{:S(2)}) copy-start(f32[1,2,1024]{2,1,0:T(2,128)} %residual.1) | copy-start | bytes 24580
  7.5 0.7 %copy-start.7 = (s32[1,1024]{1,0:T(1,128)S(1)}, s32[1,1024]{1,0:T(1,128)}, u32[]{:S(2)}) copy-start(s32[1,1024]{1,0:T(1,128)} %receiver.1) | copy-start | bytes 12292
  8.2 0.7 %copy-start.10 = (s32[1,16]{1,0:T(1,128)S(1)}, s32[1,16]{1,0:T(1,128)}, u32[]{:S(2)}) copy-start(s32[1,16]{1,0:T(1,128)} %source.1) | copy-start | bytes 196

commit v2 on v1

--- a/solution.py
+++ b/solution.py
@@ -13,6 +13,7 @@
 CENTRE = -205.0 / 72.0
 STENCIL = (1.6, -0.2, 8.0 / 315.0, -1.0 / 560.0)
 XB = 8
+OPERANDS = 12
 HALO = 8
 MESH = pl.DeviceIdType.MESH
 F32 = jnp.float32
@@ -67,24 +68,23 @@
 def kernel(
     shots,
     slabs,
-    vel,
-    fwd,
-    adj,
-    anchor,
-    source,
-    wavelet,
-    count,
-    receiver,
-    residual,
-    left_m,
-    beside_m,
-    right_m,
+    *refs,
+):
+    operands, refs = refs[:OPERANDS], refs[OPERANDS:]
+    out, held, rest = refs[0], refs[1 : 1 + OPERANDS], refs[1 + OPERANDS :]
+    compute(shots, slabs, operands, held, out, *rest)
+
+
+def compute(
+    shots,
+    slabs,
+    operands,
+    held,
     out,
+    load_sem,
     field_h,
     field_l,
     halo,
-    halo_h,
-    halo_l,
     lap,
     inj,
     hot,
@@ -103,6 +103,8 @@
     own_sum,
     slab_send,
     slab_recv,
+    moved_send,
+    moved_recv,
     flag_send,
     flag_recv,
     side_send,
@@ -116,6 +118,14 @@
     col_send,
     col_recv,
 ):
+    loads = [
+        pltpu.make_async_copy(src, dst, load_sem.at[i])
+        for i, (src, dst) in enumerate(zip(operands, held))
+    ]
+    vel, fwd, adj, anchor, source, wavelet, count, receiver, residual = held[:9]
+    left_m, beside_m, right_m = held[9:]
+    for load in loads:
+        load.start()
     tile_x, depth, tile_y = vel.shape[1:]
     along_x, plane = fwd.shape[1], fwd.shape[3]
     blocks = along_x // XB
@@ -177,10 +187,6 @@
         def _():
             copy_to(side_name, *parts).wait_send()
 
-    row_up = (home_row - anchor[0, 0]).astype(F32)
-    col_left = (home_col - anchor[0, 1]).astype(F32)
-    flag_own[...] = jnp.full(flag_own.shape, col_left, F32)
-
     for name in has:
 
         @pl.when(has[name])
@@ -214,6 +220,12 @@
     field_l[:, :4] = edge
     field_h[:, along_x + 4 :] = edge
     field_l[:, along_x + 4 :] = edge
+
+    loads[0].wait()
+    loads[3].wait()
+    row_up = (home_row - anchor[0, 0]).astype(F32)
+    col_left = (home_col - anchor[0, 1]).astype(F32)
+    flag_own[...] = jnp.full(flag_own.shape, col_left, F32)
 
     total = sum(has[name].astype(jnp.int32) for name in has)
     pl.semaphore_wait(pltpu.get_barrier_semaphore(), total)
@@ -287,6 +299,8 @@
         for name in ("left", "right"):
             start(*side_copy(name, k))
         if k == 0:
+            for load in loads[1:3]:
+                load.wait()
             for index, src in enumerate((fwd.at[0], adj.at[0])):
                 for name in ("above", "below"):
                     start(*slab_copy(name, index, src))
@@ -306,18 +320,14 @@
         def _(b):
             split_to(field_h, field_l, index, pl.ds(b * XB + 4, XB), src[0, pl.ds(b * XB, XB)])
 
-    def split_halo(index):
-        @pl.loop(0, blocks)
-        def _(b):
-            at = pl.ds(b * XB, XB)
-            split_to(halo_h, halo_l, index % 2, at, halo[index, at])
-
-    def laplace(index, b):
+    def laplace(index, b, beside):
         wide = pl.ds(b * XB, XB + 8)
         shape = ((XB + 8) * depth, plane)
         block = (field_h[index, wide].reshape(shape), field_l[index, wide].reshape(shape))
         at = pl.ds(b * XB, XB)
-        near = (halo_h[index, at].reshape(rows, plane), halo_l[index, at].reshape(rows, plane))
+        near = halo[beside, at].reshape(rows, plane)
+        near_h = near.astype(BF16)
+        near = (near_h, (near - near_h.astype(F32)).astype(BF16))
         inner = tuple(part[4 * depth : 4 * depth + rows] for part in block)
         summed = dot3((left_m[0], left_m[1]), block)
         summed = summed + dot3((beside_m[0], beside_m[1]), near)
@@ -327,7 +337,7 @@
     def first_laplace(index):
         @pl.loop(0, blocks)
         def _(b):
-            lap[index, pl.ds(b * XB, XB)] = laplace(index, b)
+            lap[index, pl.ds(b * XB, XB)] = laplace(index, b, index)
 
     first_layer = layer * depth
     total_depth = depth * slabs
@@ -378,6 +388,8 @@
         for name in ("up", "down"):
             start(*picked_copy(name, k))
 
+    for load in loads[4:]:
+        load.wait()
     split_field(0, fwd)
     split_field(1, adj)
     lane = lax.broadcasted_iota(jnp.int32, source.shape, 1)
@@ -387,7 +399,6 @@
     for index in range(2):
         for name in ("above", "below"):
             arrived(*slab_copy(name, index, (fwd, adj)[index].at[0]))
-        split_halo(index)
     first_laplace(0)
     pass_on(1)
     injections(1, receiver[...], (residual[0, 1:2], residual[0, 0:1]))
@@ -398,8 +409,6 @@
         pass_on(k)
     for name in ("up", "down"):
         arrived(*straight_copy(name))
-        for k in range(chunks):
-            arrived(*picked_copy(name, k))
 
     shape = (XB, depth, tile_y)
     is_left = mask_of(jnp.full(shape, col_left, F32), shape)
@@ -417,10 +426,22 @@
         )
         return speeds * speeds
 
-    for part_row in range(2):
-
-        @pl.loop(0, chunks)
-        def _(k):
+    def moved_copy(name, index, b):
+        layers = slice(0, HALO) if name == "above" else slice(depth - HALO, depth)
+        way = 0 if name == "above" else 1
+        at = pl.ds(b * XB, XB)
+        return (
+            name,
+            moved.at[index, at, layers, :],
+            halo.at[2 + index, at, layers, :],
+            moved_send.at[index, way, b],
+            moved_recv.at[index, way, b],
+        )
+
+    for k in range(chunks):
+        for name in ("up", "down"):
+            arrived(*picked_copy(name, k))
+        for part_row in range(2):
             squares = coefficient(part_row, k)
             x = part_row * tile_x + k * XB
             at = pl.ds(x, XB)
@@ -430,45 +451,23 @@
                 later = src[0, at] + change
                 moved[index, at] = later
                 split_to(field_h, field_l, index, pl.ds(x + 4, XB), later)
-
-    for index in range(2):
-        for name in ("above", "below"):
-            start(*slab_copy(name, 2 + index, moved.at[index]))
-    for index in range(2):
-        for name in ("above", "below"):
-            arrived(*slab_copy(name, 2 + index, moved.at[index]))
-        split_halo(2 + index)
+                for name in ("above", "below"):
+                    start(*moved_copy(name, index, part_row * chunks + k))
 
     def image(part_row, k):
         squares = coefficient(part_row, k)
         x = part_row * tile_x + k * XB
         b = part_row * chunks + k
         at = pl.ds(x, XB)
-        second = squares * laplace(0, b) + inj[1, at]
-        back = squares * laplace(1, b) + inj[3, at]
+        second = squares * laplace(0, b, 2) + inj[1, at]
+        back = squares * laplace(1, b, 3) + inj[3, at]
         later = moved[1, at]
         earlier = 2.0 * later - adj[0, at] + back
         whole = earlier * lap[0, at] + later * second
         low, high = whole[:, :, :tile_y], whole[:, :, tile_y:]
         return jnp.where(is_left, high, low), jnp.where(is_left, low, high)
 
-    for k in range(chunks):
-        at = chunk_of(k)
-        first_same, first_other = image(0, k)
-        last_same, last_other = image(1, k)
-        send_row[1, 0, at] = jnp.where(is_up, first_other, 0.0)
-        send_row[0, 0, at] = jnp.where(is_up, 0.0, last_other)
-        send_row[1, 1, at] = jnp.where(is_up, first_same, 0.0)
-        send_row[0, 1, at] = jnp.where(is_up, 0.0, last_same)
-        for part in range(2):
-            for name in ("up", "down"):
-                start(*row_copy(name, part, k))
-        own_sum[at] = jnp.where(is_up, last_same, first_same)
-        own_other = jnp.where(is_up, last_other, first_other)
-        send_col[1, at] = jnp.where(is_left, own_other, 0.0)
-        send_col[0, at] = jnp.where(is_left, 0.0, own_other)
-
-    for k in range(chunks):
+    def along_row(k):
         at = chunk_of(k)
         for name in ("up", "down"):
             arrived(*row_copy(name, 0, k))
@@ -479,6 +478,30 @@
             send_col[0, at] = send_col[0, at] + jnp.where(picks, 0.0, piece)
         for name in ("left", "right"):
             start(*col_copy(name, k))
+
+    for k in range(chunks):
+        at = chunk_of(k)
+        for part_row in range(2):
+            for index in range(2):
+                for name in ("above", "below"):
+                    arrived(*moved_copy(name, index, part_row * chunks + k))
+        first_same, first_other = image(0, k)
+        last_same, last_other = image(1, k)
+        send_row[1, 0, at] = jnp.where(is_up, first_other, 0.0)
+        send_row[0, 0, at] = jnp.where(is_up, 0.0, last_other)
+        for name in ("up", "down"):
+            start(*row_copy(name, 0, k))
+        send_row[1, 1, at] = jnp.where(is_up, first_same, 0.0)
+        send_row[0, 1, at] = jnp.where(is_up, 0.0, last_same)
+        for name in ("up", "down"):
+            start(*row_copy(name, 1, k))
+        own_sum[at] = jnp.where(is_up, last_same, first_same)
+        own_other = jnp.where(is_up, last_other, first_other)
+        send_col[1, at] = jnp.where(is_left, own_other, 0.0)
+        send_col[0, at] = jnp.where(is_left, 0.0, own_other)
+        if k:
+            along_row(k - 1)
+    along_row(chunks - 1)
     for k in range(chunks):
         at = chunk_of(k)
         for name in ("up", "down"):
@@ -502,7 +525,8 @@
     for index in range(2):
         for name in ("above", "below"):
             sent(*slab_copy(name, index, (fwd, adj)[index].at[0]))
-            sent(*slab_copy(name, 2 + index, moved.at[index]))
+            for b in range(blocks):
+                sent(*moved_copy(name, index, b))
 
 
 def body(shots, slabs, velocity, fwd_field, adj_field, anchor, source, wavelet, count, receiver, residual):
@@ -511,7 +535,11 @@
     chunks = tile_x // XB
     left_m, beside_m, right_m = (jnp.asarray(m) for m in stencil_matrices(depth, plane))
     vmem = pl.BlockSpec(memory_space=pltpu.VMEM)
-    smem = pl.BlockSpec(memory_space=pltpu.SMEM)
+    operands = (
+        velocity, fwd_field, adj_field, anchor, source, wavelet, count, receiver, residual,
+        left_m, beside_m, right_m,
+    )
+    scalars = (3, 6)
     aperture = (along_x, depth, plane)
     tile = (tile_x, depth, tile_y)
     dma = pltpu.SemaphoreType.DMA
@@ -519,14 +547,17 @@
     return pl.pallas_call(
         functools.partial(kernel, shots, slabs),
         out_shape=jax.ShapeDtypeStruct(velocity.shape, F32),
-        in_specs=[vmem, vmem, vmem, smem, vmem, vmem, smem, vmem, vmem, vmem, vmem, vmem],
+        in_specs=[pl.BlockSpec(memory_space=pltpu.HBM)] * OPERANDS,
         out_specs=vmem,
         scratch_shapes=[
+            (pltpu.SMEM if i in scalars else pltpu.VMEM)(operand.shape, operand.dtype)
+            for i, operand in enumerate(operands)
+        ]
+        + [
+            dma((OPERANDS,)),
             pltpu.VMEM((2, along_x + 8, depth, plane), BF16),
             pltpu.VMEM((2, along_x + 8, depth, plane), BF16),
             pltpu.VMEM((4,) + aperture, F32),
-            pltpu.VMEM((2,) + aperture, BF16),
-            pltpu.VMEM((2,) + aperture, BF16),
             pltpu.VMEM((2,) + aperture, F32),
             pltpu.VMEM((4,) + aperture, F32),
             pltpu.VMEM((4 * plane, lanes), BF16),
@@ -543,8 +574,10 @@
             pltpu.VMEM((2,) + tile, F32),
             pltpu.VMEM((2,) + tile, F32),
             pltpu.VMEM(tile, F32),
-            dma((4, 2)),
-            dma((4, 2)),
+            dma((2, 2)),
+            dma((2, 2)),
+            dma((2, 2, 2 * chunks)),
+            dma((2, 2, 2 * chunks)),
             dma((2,)),
             dma((2,)),
             dma((2, chunks)),
@@ -559,12 +592,9 @@
             dma((2, chunks)),
         ],
         compiler_params=pltpu.CompilerParams(
-            collective_id=0, has_side_effects=True, vmem_limit_bytes=48 * 1024 * 1024
+            collective_id=0, has_side_effects=True, vmem_limit_bytes=60 * 1024 * 1024
         ),
-    )(
-        velocity, fwd_field, adj_field, anchor, source, wavelet, count, receiver, residual,
-        left_m, beside_m, right_m,
-    )
+    )(*operands)
 
 
 def solution(mesh):

time: 51.1 us -> 40.9 us (0.80)
  the two profiles are of different devices: /device:TPU:3 before, /device:TPU:0 now
where the time goes in v2:
time: 40.9 us; the launch traced here: 40.8 us
  Pallas kernels  38.4 us (94%)
  local copies, waits for them, and re-layouts  1.67 us (4%)
  between operations  0.66 us (2%)
    pallas_call x1, Pallas kernels, body(): pl.pallas_call(functools.partial(kernel, shots, slabs), out_shape=jax.Sha...  38.4 us
    unnamed x1, local copies, waits for them, and re-layouts  1.67 us

profile of v2, /device:TPU:0, one launch (start us, length us, event | category | flops | bytes accessed | tf_op | source)
XLA Modules:
  0.0 40.8 jit_solution(4071131844485040025)
XLA Ops:
  0.7 38.4 %shard_map.118 = f32[1,32,16,128]{3,2,1,0:T(8,128)} custom-call(f32[1,32,16,128]{3,2,1,0:T(8,128)} %refs_0_.1, f32[1,64,16,256]{3,2,1,0:T(8,128)} %refs_1_.1, f32[1,64,16,256]{3,2,1,0:T(8,128)} %refs_2_.1, s32[1,2]{1,0:T(1,128)} %refs_3_.1, s32[1,16]{1,0:T(1,128)} %refs_4_.1, f32[1,2,16]{2,1,0:T(2,128)} %refs_5_.1, s32[1]{0:T(128)S(6)} %copy.14.refs_6_, ...), custom_call_target="tpu_custom_call" | custom-call | tf_op jit(solution)/shard_map/pallas_call | solution.py:547
  39.1 1.7 %copy.15 = f32[1,32,16,128]{3,2,1,0:T(8,128)} copy(f32[1,32,16,128]{3,2,1,0:T(8,128)} %shard_map.118) | data formatting | bytes 524288

commit v3 on v2

--- a/solution.py
+++ b/solution.py
@@ -509,7 +509,7 @@
         for name in ("left", "right"):
             arrived(*col_copy(name, k))
         summed = own_sum[at] + got_row[0, 1, at] + got_row[1, 1, at]
-        out[0, at] = 2.0 * vel[0, at] * (summed + got_col[0, at] + got_col[1, at])
+        out[0, at] = summed + got_col[0, at] + got_col[1, at]
 
     for name in ("up", "down"):
         sent(*flag_copy(name))
@@ -544,7 +544,7 @@
     tile = (tile_x, depth, tile_y)
     dma = pltpu.SemaphoreType.DMA
     lanes = receiver.shape[1]
-    return pl.pallas_call(
+    summed = pl.pallas_call(
         functools.partial(kernel, shots, slabs),
         out_shape=jax.ShapeDtypeStruct(velocity.shape, F32),
         in_specs=[pl.BlockSpec(memory_space=pltpu.HBM)] * OPERANDS,
@@ -595,6 +595,7 @@
             collective_id=0, has_side_effects=True, vmem_limit_bytes=60 * 1024 * 1024
         ),
     )(*operands)
+    return 2.0 * velocity * summed
 
 
 def solution(mesh):

time: 40.9 us -> 41 us (level)
  other arithmetic: 0 us -> 1.69 us
  local copies, waits for them, and re-layouts: 1.67 us -> 0.01 us
    mul x0 -> x1, other arithmetic: none -> 1.69 us  [body(): return 2.0 * velocity * summed]
    unnamed x1 -> x2, local copies, waits for them, and re-layouts: 1.67 us -> 0.01 us
where the time goes in v3:
time: 41 us; the launch traced here: 40.8 us
  Pallas kernels  38.4 us (94%)
  other arithmetic  1.69 us (4%)
  between operations  0.68 us (2%)
    pallas_call x1, Pallas kernels, body(): pl.pallas_call(functools.partial(kernel, shots, slabs), out_shape=jax.Sha...  38.4 us
    mul x1, other arithmetic, body(): return 2.0 * velocity * summed  1.69 us

profile of v3, /device:TPU:0, one launch (start us, length us, event | category | flops | bytes accessed | tf_op | source)
XLA Modules:
  0.0 40.8 jit_solution(4788794361415663242)
XLA Ops:
  0.7 0.0 copy-start
  0.7 38.4 %shard_map.118 = f32[1,32,16,128]{3,2,1,0:T(8,128)} custom-call(f32[1,32,16,128]{3,2,1,0:T(8,128)} %refs_0_.1, f32[1,64,16,256]{3,2,1,0:T(8,128)} %refs_1_.1, f32[1,64,16,256]{3,2,1,0:T(8,128)} %refs_2_.1, s32[1,2]{1,0:T(1,128)} %refs_3_.1, s32[1,16]{1,0:T(1,128)} %refs_4_.1, f32[1,2,16]{2,1,0:T(2,128)} %refs_5_.1, s32[1]{0:T(128)S(6)} %copy.13.refs_6_, ...), custom_call_target="tpu_custom_call" | custom-call | tf_op jit(solution)/shard_map/pallas_call | solution.py:547
  39.1 0.0 copy-done
  39.1 1.7 %multiply_multiply_fusion = f32[1,32,16,128]{3,2,1,0:T(8,128)} fusion(f32[1,32,16,128]{3,2,1,0:T(8,128)} %shard_map.118, f32[1,32,16,128]{3,2,1,0:T(8,128)S(1)} %copy-done), kind=kLoop, calls=%fused_computation | loop fusion | flops 131072 | bytes 786432 | tf_op jit(solution)/shard_map/mul | solution.py:598
Async XLA Ops:
  0.7 38.5 %copy-start = (f32[1,32,16,128]{3,2,1,0:T(8,128)S(1)}, f32[1,32,16,128]{3,2,1,0:T(8,128)}, u32[]{:S(2)}) copy-start(f32[1,32,16,128]{3,2,1,0:T(8,128)} %refs_0_.1) | copy-start | bytes 786436
